TPU v7x, 32 devices: a whole 2x2x4 slice. The times are simulated.
32 devices in a mesh: groups: 2 (over x), cuts: 8 (over z, y), expert: 2 (over core).
Axes of the slice: x: 2, y: 2, z: 4, core: 2. Of those that a mesh axis runs over, the one named last changes fastest.
Arguments:
- tokens: bfloat16 [4096, 3072], P(('groups', 'cuts', 'expert')), parts along dimension 0, may hold values from -6 to 6
- expert_ids: int32 [4096, 2], P(('groups', 'cuts', 'expert')), parts along dimension 0, may hold values from 0 to 7, as said below
- gate_scale: float32 [4096, 2], P(('groups', 'cuts', 'expert')), parts along dimension 0, may hold values from 0.1 to 0.9
- w_gate: bfloat16 [2, 3072, 16384], P('expert', None, 'cuts'), may hold values from -0.109375 to 0.109375
- w_up: bfloat16 [2, 3072, 16384], P('expert', None, 'cuts'), may hold values from -0.109375 to 0.109375
- w_down: bfloat16 [2, 16384, 3072], P('expert', 'cuts'), may hold values from -0.046875 to 0.046875
Outputs:
- moe_out: bfloat16 [4096, 3072], P(('groups', 'cuts', 'expert')), parts along dimension 0
There are 2 independent parts, one for each index of `groups`. A program takes and returns all parts, laid end to end along the dimension named above; an argument that names none is the same for every part. Nothing has to cross between parts.
Inputs may be any that keep to these rules, and one draw needn't show every extreme that they name: `expert_ids`: each token names two different experts. In the 128 rows of one device at most 32 name any one expert below 2; in every draw one such expert is named by exactly 32 rows on every device.
All inputs are finite; a program needn't handle non-finite values.
Results may differ from a plain program's by a relative error of at most 0.0058.
Values may be sent and summed in bfloat16 or wider, within the bound.
A program may use at most 128 MiB of HBM per device.

v0:
```python
import jax
import jax.numpy as jnp
from jax import lax
from jax.sharding import PartitionSpec as P

CAP = 32


def routing(expert_ids, gate_scale, width, capacity):
    experts = jnp.arange(width, dtype=jnp.int32)
    named = expert_ids[:, :, None] == experts[None, None, :]
    member = jnp.any(named, axis=1).astype(jnp.int32)
    weight = jnp.sum(jnp.where(named, gate_scale[:, :, None], jnp.float32(0.0)), axis=1)
    before = jnp.cumsum(member, axis=0) - member
    slots = jnp.arange(capacity, dtype=jnp.int32)
    select = (member[:, :, None] == 1) & (before[:, :, None] == slots[None, None, :])
    return (select.reshape(member.shape[0], width * capacity), weight)


def on_device(tokens, expert_ids, gate_scale, w_gate, w_up, w_down):
    width = lax.axis_size("expert")
    tok_rows = tokens.shape[0]
    features = tokens.shape[1]
    capacity = CAP
    select, weight = routing(expert_ids, gate_scale, width, capacity)
    buffer = jnp.dot(select.astype(jnp.bfloat16).T, tokens, preferred_element_type=jnp.float32)
    buffer = buffer.astype(jnp.bfloat16).reshape(width, capacity, features)
    arrived = lax.all_to_all(buffer, "expert", split_axis=0, concat_axis=0, tiled=True)
    flat_rows = lax.all_gather(arrived, "cuts", axis=0, tiled=True).reshape(-1, features)
    gate = jnp.dot(flat_rows, w_gate[0], preferred_element_type=jnp.float32)
    lin = jnp.dot(flat_rows, w_up[0], preferred_element_type=jnp.float32)
    hidden = (jax.nn.gelu(gate, approximate=False) * lin).astype(jnp.bfloat16)
    block_rows = width * capacity
    reduced = lax.psum_scatter(
        jnp.dot(hidden, w_down[0], preferred_element_type=jnp.float32),
        "cuts",
        scatter_dimension=0,
        tiled=True,
    )
    reduced = reduced.astype(jnp.bfloat16).reshape(width, capacity, features)
    expert_rows = lax.all_to_all(reduced, "expert", split_axis=0, concat_axis=0, tiled=True)
    coef = select.astype(jnp.float32).reshape(tok_rows, width, capacity) * weight[:, :, None]
    combined = jnp.dot(
        coef.reshape(tok_rows, block_rows),
        expert_rows.reshape(block_rows, features).astype(jnp.float32),
        precision=lax.Precision.HIGHEST,
    )
    return combined.astype(jnp.bfloat16)


def solution(mesh):
    placed = (
        P(("groups", "cuts", "expert"), None),
        P(("groups", "cuts", "expert"), None),
        P(("groups", "cuts", "expert"), None),
        P("expert", None, "cuts"),
        P("expert", None, "cuts"),
        P("expert", "cuts", None),
    )
    return jax.shard_map(
        on_device,
        mesh=mesh,
        in_specs=placed,
        out_specs=P(("groups", "cuts", "expert"), None),
        check_vma=False,
    )
```

profile of v0, /device:TPU:0, one launch (start us, length us, event | category | flops | bytes accessed | tf_op | source)
XLA Modules:
  0.0 253.6 jit_solution(5910473007096470929)
XLA Ops:
  6.5 0.0 copy-start
  6.5 0.0 all-gather.2.cloned.1.call-start
  6.5 0.8 fusion.60
  7.3 0.1 copy.19
  7.4 0.2 reduce_window_sum.11
  7.6 0.1 copy.20
  7.7 0.1 eq.59
  7.8 0.1 fusion.55
  7.9 0.0 copy-done
  7.9 0.3 convolution_convert_fusion
  8.1 4.8 %all_to_all.10 = bf16[2,32,3072]{2,1,0:T(8,128)(2,1)} all-to-all(bf16[2,32,3072]{2,1,0:T(8,128)(2,1)S(1)} %bitcast.31), channel_id=1, replica_groups=mesh['groups'=2,'cuts'=8,'expert'=2] {'expert'}, dimensions={0} | all-to-all | bytes 786432 | tf_op jit(solution)/shard_map/all_to_all | solution.py:28
  12.9 0.0 all-gather.2.cloned.1.call-update
  12.9 0.0 reduce-scatter.2.cloned.1.call-start
  13.0 63.3 %all-gather.2.cloned.1.call-done = bf16[16,32,3072]{2,1,0:T(8,128)(2,1)} async-done(((bf16[2,32,3072]{2,1,0:T(8,128)(2,1)}), bf16[16,32,3072]{2,1,0:T(8,128)(2,1)}) %all-gather.2.cloned.1.call-update) | async-done | bytes 3145744 | tf_op jit(solution)/shard_map/all_gather | solution.py:29
  76.3 11.9 %fusion.4 = f32[512,2048]{1,0:T(8,128)} fusion(bf16[512,3072]{1,0:T(8,128)(2,1)} %bitcast.33, bf16[1,3072,2048]{2,1,0:T(8,128)(2,1)} %param.9), kind=kOutput, calls=%fused_computation.4 | convolution fusion | flops 6442450944 | bytes 19922944 | tf_op jit(solution)/shard_map/dot_general | solution.py:30
  88.2 34.9 %fusion = f32[512,3072]{1,0:T(8,128)} fusion(bf16[1,2048,3072]{2,1,0:T(8,128)(2,1)} %param.11, f32[512,2048]{1,0:T(8,128)} %fusion.4, bf16[512,3072]{1,0:T(8,128)(2,1)} %bitcast.34, bf16[1,3072,2048]{2,1,0:T(8,128)(2,1)} %param.10), kind=kOutput, calls=%fused_computation | convolution fusion | flops 12954107904 | bytes 38797312 | tf_op jit(solution)/shard_map/dot_general | solution.py:35
  123.0 0.0 copy-start.1
  123.0 0.0 copy-start.2
  123.0 0.0 reduce-scatter.2.cloned.1.call-update
  123.0 0.7 copy-done.1
  123.7 0.0 copy-done.2
  123.7 116.1 %reduce-scatter.2.cloned.1.call-done = f32[64,3072]{1,0:T(8,128)} async-done(((f32[512,3072]{1,0:T(8,128)}), f32[64,3072]{1,0:T(8,128)}) %reduce-scatter.2.cloned.1.call-update) | async-done | bytes 786448 | tf_op jit(solution)/shard_map/reduce_scatter | solution.py:34
  239.8 1.2 convert_element_type.33
  241.0 4.0 %all_to_all.11 = bf16[2,32,3072]{2,1,0:T(8,128)(2,1)S(1)} all-to-all(bf16[2,32,3072]{2,1,0:T(8,128)(2,1)S(1)} %bitcast.32), channel_id=1, replica_groups=mesh['groups'=2,'cuts'=8,'expert'=2] {'expert'}, dimensions={0} | all-to-all | bytes 786432 | tf_op jit(solution)/shard_map/all_to_all | solution.py:41
  245.0 1.7 fusion.17
  (4 shorter events, 0.0 us)
Async XLA Ops:
  6.5 1.3 copy-start
  6.5 69.7 %all-gather.2.cloned.1.call-start = ((), (), s32[]{:S(2)}) async-start(), calls=%async_computation.3 | async-start | bytes 3538944 | tf_op jit(solution)/shard_map/all_gather | solution.py:29
  12.9 226.8 %reduce-scatter.2.cloned.1.call-start = ((), (), s32[]{:S(2)}) async-start(), calls=%async_computation.4 | async-start | bytes 7077888 | tf_op jit(solution)/shard_map/reduce_scatter | solution.py:34
  123.0 0.7 copy-start.1
  123.0 0.7 copy-start.2
Sparse Core Ops, SparseCore 0:
  13.1 63.1 all-gather.1
  123.2 116.5 reduce-scatter.1
where the time goes:
time: 254 us
  waiting for transfers between devices  179 us (70%)
  matrix products  48.7 us (19%)
  between operations  13.4 us (5%)
  blocking collectives  8.83 us (3%)
    reduce_scatter x1, waiting for transfers between devices, on_device(): lax.psum_scatter(jnp.dot(hidden, w_down[0], preferred_element_type=jnp.fl...  116 us
    all_gather x1, waiting for transfers between devices, on_device(): lax.all_gather(arrived, 'cuts', axis=0, tiled=True).reshape(-1, features)  63.3 us
    dot_general x1, matrix products, on_device(): jnp.dot(hidden, w_down[0], preferred_element_type=jnp.float32)  34.9 us
    dot_general x1, matrix products, on_device(): gate = jnp.dot(flat_rows, w_gate[0], preferred_element_type=jnp.float32)  11.9 us
  transfers between devices with their start and end apart: 2, of which 2 were waited for; matrix products, arithmetic and copies ran while one was open for 0% of the time, Pallas kernels for 0%

commit v1 on v0

v1 whole, which is shorter than its diff:
```python
import functools

import jax
import jax.numpy as jnp
from jax import lax
from jax.experimental import pallas as pl
from jax.experimental.pallas import tpu as pltpu
from jax.sharding import PartitionSpec as P

CAP = 32
SUB = 2
TILE = 256
MESH = pl.DeviceIdType.MESH


def ring_place(cut, n):
    side = cut % 2
    row = cut // 2
    return row + side * (n - 1 - 2 * row)


def ring_cut(place, n):
    back = place // (n // 2)
    return (1 - back) * (2 * place) + back * (2 * (n - 1 - place) + 1)


def kernel(n, tok, ids, gates, w_gate, w_up, w_down, out, wg, wu, wd, x, part, acc, fin, stage, hidden,
           w_sem, swap_send, swap_recv, ag_send, ag_recv, rs_send, rs_recv):
    half = n // 2
    core = lax.axis_index("expert")
    other = 1 - core
    place = ring_place(lax.axis_index("cuts"), n)
    right = ring_cut((place + 1) % n, n)
    left = ring_cut((place + n - 1) % n, n)
    toward = (right, left)

    barrier = pltpu.get_barrier_semaphore()
    for who in ({"expert": other}, {"cuts": right}, {"cuts": left},
                {"cuts": right, "expert": other}, {"cuts": left, "expert": other}):
        pl.semaphore_signal(barrier, inc=1, device_id=who, device_id_type=MESH)

    loads = []
    for at, (src, dst) in enumerate(((w_gate, wg), (w_up, wu), (w_down, wd))):
        rows = dst.shape[0] // 2
        pair = []
        for k in range(2):
            copy = pltpu.make_async_copy(src.at[0, pl.ds(k * rows, rows)], dst.at[pl.ds(k * rows, rows)], w_sem.at[at, k])
            copy.start()
            pair.append(copy)
        loads.append(pair)

    count = tok.shape[0]
    id_a, id_b = ids[:, 0:1], ids[:, 1:2]
    ga, gb = gates[:, 0:1], gates[:, 1:2]
    rows_at = lax.broadcasted_iota(jnp.int32, (count, count), 0)
    cols_at = lax.broadcasted_iota(jnp.int32, (count, count), 1)
    lower = jnp.where(cols_at < rows_at, 1.0, 0.0).astype(jnp.bfloat16)
    lanes = lax.broadcasted_iota(jnp.int32, (count, 128), 1)
    select = jnp.zeros((count, 128), jnp.float32)
    weights = []
    for at, e in enumerate((core, other)):
        hit_a, hit_b = id_a == e, id_b == e
        member = jnp.where(hit_a, 1.0, 0.0) + jnp.where(hit_b, 1.0, 0.0)
        weights.append(jnp.where(hit_a, ga, 0.0) + jnp.where(hit_b, gb, 0.0))
        member = jnp.broadcast_to(member, (count, 128))
        before = jnp.dot(lower, member.astype(jnp.bfloat16), preferred_element_type=jnp.float32)
        hit = (before + (at * CAP)) == lanes.astype(jnp.float32)
        inside = jnp.where(lanes >= at * CAP, 1.0, 0.0) * jnp.where(lanes < (at + 1) * CAP, 1.0, 0.0)
        select = select + jnp.where(hit, member, 0.0) * inside
    gather = select.T.astype(jnp.bfloat16)[: 2 * CAP]
    buf = jnp.dot(gather, tok[...], preferred_element_type=jnp.float32).astype(jnp.bfloat16)
    x[0, 0, 0] = buf[:CAP]
    stage[0] = buf[CAP:]

    pl.semaphore_wait(barrier, 5)

    started = []

    def remote(src, dst, ssem, rsem, who):
        return pltpu.make_async_remote_copy(src_ref=src, dst_ref=dst, send_sem=ssem, recv_sem=rsem,
                                            device_id=who, device_id_type=MESH)

    def xref(t, d, s):
        return x.at[t // 2, t % 2, d, pl.ds(s * (CAP // SUB), CAP // SUB)]

    def ag_copy(t, d, s):
        if t == 1:
            src = xref(0, d, s)
        elif t == half + 1:
            src = xref(0, 1 - d, s)
        else:
            src = xref(t - 1, d, s)
        return remote(src, xref(t, d, s), ag_send.at[d, t, s], ag_recv.at[d, t, s], {"cuts": toward[d]})

    def ag_start(t, d, s):
        copy = ag_copy(t, d, s)
        copy.start()
        started.append(copy)

    swap = remote(stage.at[0], x.at[0, 0, 1], swap_send.at[0], swap_recv.at[0], {"expert": other})
    swap.start()
    started.append(swap)
    for s in range(SUB):
        ag_start(1, 0, s)
    swap.wait_recv()
    for s in range(SUB):
        ag_start(1, 1, s)

    def ag(t):
        for s in range(SUB):
            for d in range(2):
                ag_copy(t, d, s).wait_recv()
                if t != half and t < n - 1:
                    ag_start(t + 1, d, s)
        if t == half - 1:
            for s in range(SUB):
                for d in range(2):
                    ag_start(half + 1, d, s)

    def up_part(j):
        if j == 0:
            for pair in loads[:2]:
                for copy in pair:
                    copy.wait()

        def body(c, carry):
            cols = pl.ds(pl.multiple_of(c * TILE, TILE), TILE)
            rows = x[j].reshape(4 * CAP, x.shape[-1])
            g = jnp.dot(rows, wg[:, cols], preferred_element_type=jnp.float32)
            u = jnp.dot(rows, wu[:, cols], preferred_element_type=jnp.float32)
            h = 0.5 * g * (1.0 + lax.erf(g * 0.7071067811865476)) * u
            hidden[:, cols] = h.astype(jnp.bfloat16)
            return carry

        lax.fori_loop(0, wg.shape[1] // TILE, body, 0)

    def down_part(j):
        if j == 0:
            for copy in loads[2]:
                copy.wait()

        def body(c, carry):
            cols = pl.ds(pl.multiple_of(c * TILE, TILE), TILE)
            r = jnp.dot(hidden[...], wd[:, cols], preferred_element_type=jnp.float32)
            part[j, :, :, :, cols] = r.astype(jnp.bfloat16).reshape(2, 2, CAP, TILE)
            return carry

        lax.fori_loop(0, wd.shape[1] // TILE, body, 0)

    def pref(t, d, s):
        return part.at[t // 2, t % 2, d, pl.ds(s * (CAP // SUB), CAP // SUB)]

    def own(chain, d, k, s):
        if chain == 0:
            return pref(k, 1 - d, s)
        if k == half:
            return pref(half, d, s)
        return pref(half + k, 1 - d, s)

    def top(chain):
        return half - 1 + chain

    def aref(chain, d, k, s):
        return acc.at[chain, d, k, pl.ds(s * (CAP // SUB), CAP // SUB)]

    def fref(h, d, s):
        return fin.at[h, d, pl.ds(s * (CAP // SUB), CAP // SUB)]

    def rs_copy(chain, d, k, s):
        src = own(chain, d, k, s) if k == top(chain) else aref(chain, d, k, s)
        h = (1 - chain) if d == 0 else chain
        ssem, rsem = rs_send.at[chain, d, k, s], rs_recv.at[chain, d, k, s]
        if k > 1:
            return remote(src, aref(chain, d, k - 1, s), ssem, rsem, {"cuts": toward[d]})
        if h == 0:
            return remote(src, fref(0, d, s), ssem, rsem, {"cuts": toward[d]})
        return remote(src, fref(1, d, s), ssem, rsem, {"cuts": toward[d], "expert": other})

    def rs_start(chain, d, k, s):
        copy = rs_copy(chain, d, k, s)
        copy.start()
        started.append(copy)

    def rs_open(chain):
        for s in range(SUB):
            for d in range(2):
                rs_start(chain, d, top(chain), s)

    def rs(chain, k):
        for s in range(SUB):
            for d in range(2):
                rs_copy(chain, d, k + 1, s).wait_recv()
                if k > 0:
                    a, b = aref(chain, d, k, s), own(chain, d, k, s)
                    a[...] = (a[...].astype(jnp.float32) + b[...].astype(jnp.float32)).astype(jnp.bfloat16)
                    rs_start(chain, d, k, s)

    own_swap = remote(part.at[0, 0, 1], stage.at[1], swap_send.at[1], swap_recv.at[1], {"expert": other})

    opened = 0
    for t in range(1, n):
        ag(t)
        if t >= 2 and t % 2 == 0:
            up_part(t // 2 - 1)
        if t >= 3 and t % 2 == 1:
            j = (t - 3) // 2
            down_part(j)
            if j == 0:
                own_swap.start()
                started.append(own_swap)
            if opened == 0 and 2 * j + 1 >= half - 1:
                rs_open(0)
                opened = 1
            if opened == 1 and 2 * j + 1 >= half:
                rs_open(1)
                opened = 2
    work = [functools.partial(up_part, half - 1), functools.partial(down_part, half - 1)]
    for k in range(half - 2, -1, -1):
        rs(0, k)
        if work:
            work.pop(0)()
    for item in work:
        item()
    for k in range(half - 1, -1, -1):
        rs(1, k)
    own_swap.wait_recv()

    keep = select.astype(jnp.bfloat16)
    first = fin[0, 0].astype(jnp.float32) + fin[0, 1].astype(jnp.float32) + part[0, 0, 0].astype(jnp.float32)
    second = fin[1, 0].astype(jnp.float32) + fin[1, 1].astype(jnp.float32) + stage[1].astype(jnp.float32)
    res = weights[0] * jnp.dot(keep[:, :CAP], first.astype(jnp.bfloat16), preferred_element_type=jnp.float32)
    res += weights[1] * jnp.dot(keep[:, CAP:2 * CAP], second.astype(jnp.bfloat16), preferred_element_type=jnp.float32)
    out[...] = res.astype(out.dtype)

    for copy in started:
        copy.wait_send()


def on_device(tokens, expert_ids, gate_scale, w_gate, w_up, w_down):
    n = lax.axis_size("cuts")
    half = n // 2
    feat = tokens.shape[1]
    ff = w_gate.shape[2]
    bf = jnp.bfloat16
    vmem = pl.BlockSpec(memory_space=pltpu.VMEM)
    hbm = pl.BlockSpec(memory_space=pl.ANY)
    dma = pltpu.SemaphoreType.DMA
    return pl.pallas_call(
        functools.partial(kernel, n),
        out_shape=jax.ShapeDtypeStruct(tokens.shape, bf),
        in_specs=[vmem, vmem, vmem, hbm, hbm, hbm],
        out_specs=vmem,
        scratch_shapes=[
            pltpu.VMEM((feat, ff), bf),
            pltpu.VMEM((feat, ff), bf),
            pltpu.VMEM((ff, feat), bf),
            pltpu.VMEM((half, 2, 2, CAP, feat), bf),
            pltpu.VMEM((half, 2, 2, CAP, feat), bf),
            pltpu.VMEM((2, 2, half, CAP, feat), bf),
            pltpu.VMEM((2, 2, CAP, feat), bf),
            pltpu.VMEM((2, CAP, feat), bf),
            pltpu.VMEM((4 * CAP, ff), bf),
            dma((3, 2)),
            dma((2,)),
            dma((2,)),
            dma((2, n, SUB)),
            dma((2, n, SUB)),
            dma((2, 2, half + 1, SUB)),
            dma((2, 2, half + 1, SUB)),
        ],
        compiler_params=pltpu.CompilerParams(
            collective_id=0, has_side_effects=True, vmem_limit_bytes=60 * 1024 * 1024
        ),
        name="moe_ring",
    )(tokens, expert_ids, gate_scale, w_gate, w_up, w_down)


def solution(mesh):
    placed = (
        P(("groups", "cuts", "expert"), None),
        P(("groups", "cuts", "expert"), None),
        P(("groups", "cuts", "expert"), None),
        P("expert", None, "cuts"),
        P("expert", None, "cuts"),
        P("expert", "cuts", None),
    )
    return jax.shard_map(
        on_device,
        mesh=mesh,
        in_specs=placed,
        out_specs=P(("groups", "cuts", "expert"), None),
        check_vma=False,
    )
```

time: 254 us -> 89.5 us (0.35)
  waiting for transfers between devices: 179 us -> 0 us
  Pallas kernels: 0 us -> 84.4 us
  matrix products: 48.7 us -> 0 us
  between operations: 13.4 us -> 0.01 us
  blocking collectives: 8.83 us -> 0 us
  local copies, waits for them, and re-layouts: 0.94 us -> 4.87 us
    reduce_scatter x1 -> x0, waiting for transfers between devices: 116 us -> none  [on_device(): lax.psum_scatter(jnp.dot(hidden, w_down[0], preferred_element_type=jnp.fl...]
    pallas_call x0 -> x1, Pallas kernels: none -> 84.4 us  [on_device(): pl.pallas_call(functools.partial(kernel, n), out_shape=jax.ShapeDtypeStru...]
    all_gather x1 -> x0, waiting for transfers between devices: 63.3 us -> none  [on_device(): lax.all_gather(arrived, 'cuts', axis=0, tiled=True).reshape(-1, features)]
    dot_general x4 -> x0, matrix products: 48.7 us -> none  [the longest x1 34.9 us: on_device(): jnp.dot(hidden, w_down[0], preferred_element_type=jnp.float32)]
    all_to_all x2 -> x0, blocking collectives: 8.83 us -> none  [the longest x1 4.78 us: on_device(): lax.all_to_all(buffer, 'expert', split_axis=0, concat_axis=0, tiled=True)]
    unnamed x6 -> x3, local copies, waits for them, and re-layouts: 0.67 us -> 4.87 us
  transfers between devices with their start and end apart: 2 -> 0, of which waited for: 2 -> 0; matrix products, arithmetic and copies ran while one was open for 0% -> 0% of each run, Pallas kernels for 0% -> 0%
where the time goes in v1:
time: 89.5 us; the launch traced here: 89.3 us
  Pallas kernels  84.4 us (94%)
  local copies, waits for them, and re-layouts  4.87 us (5%)
    pallas_call x1, Pallas kernels, on_device(): pl.pallas_call(functools.partial(kernel, n), out_shape=jax.ShapeDtypeStru...  84.4 us
    unnamed x3, local copies, waits for them, and re-layouts  4.87 us

profile of v1, /device:TPU:0, one launch (start us, length us, event | category | flops | bytes accessed | tf_op | source)
XLA Modules:
  0.0 89.3 jit_solution(12828629076551593901)
XLA Ops:
  0.0 1.4 %copy.7.ids = s32[128,2]{1,0:T(8,128)} copy(s32[128,2]{0,1:T(2,128)} %param.7) | data formatting | bytes 2048 | tf_op args[1]
  1.4 1.4 %copy.8.gates = f32[128,2]{1,0:T(8,128)} copy(f32[128,2]{0,1:T(2,128)} %param.8) | data formatting | bytes 2048 | tf_op args[2]
  2.8 84.4 %moe_ring.1 = bf16[128,3072]{1,0:T(8,128)(2,1)} custom-call(bf16[128,3072]{1,0:T(8,128)(2,1)} %tok.1, s32[128,2]{1,0:T(8,128)} %copy.7.ids, f32[128,2]{1,0:T(8,128)} %copy.8.gates, bf16[1,3072,2048]{2,1,0:T(8,128)(2,1)} %w_gate.1, bf16[1,3072,2048]{2,1,0:T(8,128)(2,1)} %w_up.1, bf16[1,2048,3072]{2,1,0:T(8,128)(2,1)} %w_down.1), custom_call_target="tpu_custom_call" | custom-call | tf_op jit(solution)/shard_map/moe_ring/pallas_call | solution.py:248
  87.2 2.1 %copy.10 = bf16[128,3072]{1,0:T(8,128)(2,1)} copy(bf16[128,3072]{1,0:T(8,128)(2,1)} %moe_ring.1) | data formatting | bytes 1572864

commit v2 on v1

v2 whole, which is shorter than its diff:
```python
import functools

import jax
import jax.numpy as jnp
from jax import lax
from jax.experimental import pallas as pl
from jax.experimental.pallas import tpu as pltpu
from jax.sharding import PartitionSpec as P

CAP = 32
SUB = 2
TILE = 512
UP_BITS = 2
DOWN_BITS = 2
WARM = 3
MESH = pl.DeviceIdType.MESH


def ring_place(cut, n):
    side = cut % 2
    row = cut // 2
    return row + side * (n - 1 - 2 * row)


def ring_cut(place, n):
    back = place // (n // 2)
    return (1 - back) * (2 * place) + back * (2 * (n - 1 - place) + 1)


def kernel(n, tok_hbm, ids_hbm, gates_hbm, w_gate, w_up, w_down, out_hbm, tok, ids, gates, out, wg, wu, wd, x, part, acc, fin,
           stage, hidden, in_sem, out_sem, w_sem, swap_send, swap_recv, ag_send, ag_recv, rs_send, rs_recv):
    half = n // 2
    core = lax.axis_index("expert")
    other = 1 - core
    place = ring_place(lax.axis_index("cuts"), n)
    right = ring_cut((place + 1) % n, n)
    left = ring_cut((place + n - 1) % n, n)
    toward = (right, left)

    barrier = pltpu.get_barrier_semaphore()
    for who in ({"expert": other}, {"cuts": right}, {"cuts": left},
                {"cuts": right, "expert": other}, {"cuts": left, "expert": other}):
        pl.semaphore_signal(barrier, inc=1, device_id=who, device_id_type=MESH)

    brought = [pltpu.make_async_copy(src, dst, in_sem.at[at])
               for at, (src, dst) in enumerate(((ids_hbm, ids), (gates_hbm, gates), (tok_hbm, tok)))]
    for copy in brought:
        copy.start()

    count = tok.shape[0]
    feat = tok.shape[1]
    width = feat // SUB
    rows_at = lax.broadcasted_iota(jnp.int32, (count, count), 0)
    cols_at = lax.broadcasted_iota(jnp.int32, (count, count), 1)
    upper = jnp.where(rows_at < cols_at, 1.0, 0.0).astype(jnp.bfloat16)
    brought[0].wait()

    id_a, id_b = ids[0:1, :], ids[1:2, :]
    slots = lax.broadcasted_iota(jnp.int32, (CAP, count), 0).astype(jnp.float32)
    pieces = []
    for e in (core, other):
        member = jnp.where(id_a == e, 1.0, 0.0) + jnp.where(id_b == e, 1.0, 0.0)
        member = jnp.broadcast_to(member, (CAP, count))
        before = jnp.dot(member.astype(jnp.bfloat16), upper, preferred_element_type=jnp.float32)
        pieces.append(jnp.where(before == slots, member, 0.0))
    gather = jnp.concatenate(pieces, axis=0)
    brought[2].wait()
    loads = []
    for at, (src, dst) in enumerate(((w_gate, wg), (w_up, wu), (w_down, wd))):
        rows = dst.shape[0] // 2
        pair = []
        for k in range(2):
            copy = pltpu.make_async_copy(src.at[0, pl.ds(k * rows, rows)], dst.at[pl.ds(k * rows, rows)], w_sem.at[at, k])
            copy.start()
            pair.append(copy)
        loads.append(pair)
    buf = jnp.dot(gather.astype(jnp.bfloat16), tok[...], preferred_element_type=jnp.float32).astype(jnp.bfloat16)
    x[0, 0, 0] = buf[:CAP]
    stage[0] = buf[CAP:]

    pl.semaphore_wait(barrier, 5)

    started = []

    def remote(src, dst, ssem, rsem, who):
        return pltpu.make_async_remote_copy(src_ref=src, dst_ref=dst, send_sem=ssem, recv_sem=rsem,
                                            device_id=who, device_id_type=MESH)

    def xref(t, d, s):
        return x.at[t // 2, t % 2, d, :, pl.ds(s * width, width)]

    def ag_copy(t, d, s):
        if t == 1:
            src = xref(0, d, s)
        elif t == half + 1:
            src = xref(0, 1 - d, s)
        else:
            src = xref(t - 1, d, s)
        return remote(src, xref(t, d, s), ag_send.at[d, t, s], ag_recv.at[d, t, s], {"cuts": toward[d]})

    def ag_start(t, d, s):
        copy = ag_copy(t, d, s)
        copy.start()
        started.append(copy)

    swap = remote(stage.at[0], x.at[0, 0, 1], swap_send.at[0], swap_recv.at[0], {"expert": other})
    swap.start()
    started.append(swap)
    for s in range(SUB):
        ag_start(1, 0, s)
    swap.wait_recv()
    for s in range(SUB):
        ag_start(1, 1, s)

    def ag(t, s):
        for d in range(2):
            ag_copy(t, d, s).wait_recv()
            if t != half and t < n - 1:
                ag_start(t + 1, d, s)
        if t == half - 1:
            for d in range(2):
                ag_start(half + 1, d, s)

    def up_part(j, lo, hi):
        if j == 0 and lo == 0:
            for pair in loads[:2]:
                for copy in pair:
                    copy.wait()

        def body(c, carry):
            cols = pl.ds(pl.multiple_of(c * TILE, TILE), TILE)
            rows = x[j].reshape(4 * CAP, feat)
            g = jnp.dot(rows, wg[:, cols], preferred_element_type=jnp.float32)
            u = jnp.dot(rows, wu[:, cols], preferred_element_type=jnp.float32)
            h = 0.5 * g * (1.0 + lax.erf(g * 0.7071067811865476)) * u
            hidden[:, cols] = h.astype(jnp.bfloat16)
            return carry

        lax.fori_loop(lo, hi, body, 0)

    def down_part(j, lo, hi):
        if j == 0 and lo == 0:
            for copy in loads[2]:
                copy.wait()

        def body(c, carry):
            cols = pl.ds(pl.multiple_of(c * TILE, TILE), TILE)
            r = jnp.dot(hidden[...], wd[:, cols], preferred_element_type=jnp.float32)
            part[j, :, :, :, cols] = r.astype(jnp.bfloat16).reshape(2, 2, CAP, TILE)
            return carry

        lax.fori_loop(lo, hi, body, 0)

    def pref(t, d, s):
        return part.at[t // 2, t % 2, d, :, pl.ds(s * width, width)]

    def own(chain, d, k, s):
        if chain == 0:
            return pref(k, 1 - d, s)
        if k == half:
            return pref(half, d, s)
        return pref(half + k, 1 - d, s)

    def top(chain):
        return half - 1 + chain

    def aref(chain, d, k, s):
        return acc.at[chain, d, k, :, pl.ds(s * width, width)]

    def fref(h, d, s):
        return fin.at[h, d, :, pl.ds(s * width, width)]

    def rs_copy(chain, d, k, s):
        src = own(chain, d, k, s) if k == top(chain) else aref(chain, d, k, s)
        h = (1 - chain) if d == 0 else chain
        ssem, rsem = rs_send.at[chain, d, k, s], rs_recv.at[chain, d, k, s]
        if k > 1:
            return remote(src, aref(chain, d, k - 1, s), ssem, rsem, {"cuts": toward[d]})
        if h == 0:
            return remote(src, fref(0, d, s), ssem, rsem, {"cuts": toward[d]})
        return remote(src, fref(1, d, s), ssem, rsem, {"cuts": toward[d], "expert": other})

    def rs_start(chain, d, k, s):
        copy = rs_copy(chain, d, k, s)
        copy.start()
        started.append(copy)

    def rs_open(chain):
        for s in range(SUB):
            for d in range(2):
                rs_start(chain, d, top(chain), s)

    def rs(chain, k, s):
        for d in range(2):
            rs_copy(chain, d, k + 1, s).wait_recv()
            if k > 0:
                a, b = aref(chain, d, k, s), own(chain, d, k, s)
                a[...] = (a[...].astype(jnp.float32) + b[...].astype(jnp.float32)).astype(jnp.bfloat16)
                rs_start(chain, d, k, s)

    own_swap = remote(part.at[0, 0, 1], stage.at[1], swap_send.at[1], swap_recv.at[1], {"expert": other})

    def swap_own():
        own_swap.start()
        started.append(own_swap)

    ups, downs = wg.shape[1] // TILE, feat // TILE
    bits = []
    for j in range(half):
        cuts = [ups * k // UP_BITS for k in range(UP_BITS + 1)]
        bits += [(2 * j + 1, functools.partial(up_part, j, lo, hi)) for lo, hi in zip(cuts, cuts[1:]) if lo < hi]
        cuts = [downs * k // DOWN_BITS for k in range(DOWN_BITS + 1)]
        bits += [(2 * j + 1, functools.partial(down_part, j, lo, hi)) for lo, hi in zip(cuts, cuts[1:]) if lo < hi]
        bits.append((2 * j + 1, ("pass", j)))
    done = -1
    opened = 0

    def advance(reached):
        nonlocal done, opened
        if not bits or bits[0][0] > reached:
            return False
        bits.pop(0)[1]()
        if bits and isinstance(bits[0][1], tuple):
            done = bits.pop(0)[1][1]
            if done == 0:
                swap_own()
            if opened == 0 and 2 * done + 1 >= half - 1:
                rs_open(0)
                opened = 1
            if opened == 1 and 2 * done + 1 >= half:
                rs_open(1)
                opened = 2
        return True

    for t in range(1, n):
        for s in range(SUB):
            ag(t, s)
            if t >= WARM:
                advance(t if s == SUB - 1 else t - 1)
    while opened == 0:
        advance(n - 1)
    for k in range(half - 2, -1, -1):
        for s in range(SUB):
            rs(0, k, s)
            advance(n - 1)
    while bits:
        advance(n - 1)
    for k in range(half - 1, 0, -1):
        for s in range(SUB):
            rs(1, k, s)

    gates_copy = brought[1]
    gates_copy.wait()
    keep = jnp.concatenate([gather, jnp.zeros((count - 2 * CAP, count), jnp.float32)], axis=0).T.astype(jnp.bfloat16)
    spread = []
    for e in (core, other):
        w = jnp.where(id_a == e, gates[0:1, :], 0.0) + jnp.where(id_b == e, gates[1:2, :], 0.0)
        spread.append(jnp.broadcast_to(w, (count, count)).T[:, 0:1])
    own_swap.wait_recv()
    outs = []
    for s in range(SUB):
        cols = slice(s * width, (s + 1) * width)
        rs(1, 0, s)
        first = fin[0, 0, :, cols].astype(jnp.float32) + fin[0, 1, :, cols].astype(jnp.float32) + part[0, 0, 0, :, cols].astype(jnp.float32)
        second = fin[1, 0, :, cols].astype(jnp.float32) + fin[1, 1, :, cols].astype(jnp.float32) + stage[1, :, cols].astype(jnp.float32)
        res = spread[0] * jnp.dot(keep[:, :CAP], first.astype(jnp.bfloat16), preferred_element_type=jnp.float32)
        res += spread[1] * jnp.dot(keep[:, CAP:2 * CAP], second.astype(jnp.bfloat16), preferred_element_type=jnp.float32)
        out[:, cols] = res.astype(out.dtype)
        copy = pltpu.make_async_copy(out.at[:, pl.ds(s * width, width)], out_hbm.at[:, pl.ds(s * width, width)], out_sem.at[s])
        copy.start()
        outs.append(copy)
    for copy in outs:
        copy.wait()
    for copy in started:
        copy.wait_send()


def on_device(tokens, expert_ids, gate_scale, w_gate, w_up, w_down):
    n = lax.axis_size("cuts")
    half = n // 2
    feat = tokens.shape[1]
    ff = w_gate.shape[2]
    bf = jnp.bfloat16
    hbm = pl.BlockSpec(memory_space=pl.ANY)
    dma = pltpu.SemaphoreType.DMA
    return pl.pallas_call(
        functools.partial(kernel, n),
        out_shape=jax.ShapeDtypeStruct(tokens.shape, bf),
        in_specs=[hbm] * 6,
        out_specs=hbm,
        scratch_shapes=[
            pltpu.VMEM(tokens.shape, bf),
            pltpu.VMEM((2, tokens.shape[0]), jnp.int32),
            pltpu.VMEM((2, tokens.shape[0]), jnp.float32),
            pltpu.VMEM(tokens.shape, bf),
            pltpu.VMEM((feat, ff), bf),
            pltpu.VMEM((feat, ff), bf),
            pltpu.VMEM((ff, feat), bf),
            pltpu.VMEM((half, 2, 2, CAP, feat), bf),
            pltpu.VMEM((half, 2, 2, CAP, feat), bf),
            pltpu.VMEM((2, 2, half, CAP, feat), bf),
            pltpu.VMEM((2, 2, CAP, feat), bf),
            pltpu.VMEM((2, CAP, feat), bf),
            pltpu.VMEM((4 * CAP, ff), bf),
            dma((3,)),
            dma((SUB,)),
            dma((3, 2)),
            dma((2,)),
            dma((2,)),
            dma((2, n, SUB)),
            dma((2, n, SUB)),
            dma((2, 2, half + 1, SUB)),
            dma((2, 2, half + 1, SUB)),
        ],
        compiler_params=pltpu.CompilerParams(
            collective_id=0, has_side_effects=True, vmem_limit_bytes=60 * 1024 * 1024
        ),
        name="moe_ring",
    )(tokens, expert_ids.T, gate_scale.T, w_gate, w_up, w_down)


def solution(mesh):
    placed = (
        P(("groups", "cuts", "expert"), None),
        P(("groups", "cuts", "expert"), None),
        P(("groups", "cuts", "expert"), None),
        P("expert", None, "cuts"),
        P("expert", None, "cuts"),
        P("expert", "cuts", None),
    )
    return jax.shard_map(
        on_device,
        mesh=mesh,
        in_specs=placed,
        out_specs=P(("groups", "cuts", "expert"), None),
        check_vma=False,
    )
```

time: 89.5 us -> 77 us (0.86)
  Pallas kernels: 84.4 us -> 74 us
  local copies, waits for them, and re-layouts: 4.87 us -> 2.06 us
    pallas_call x1, Pallas kernels: 84.4 us -> 74 us  [on_device(): pl.pallas_call(functools.partial(kernel, n), out_shape=jax.ShapeDtypeStru...]
    unnamed x3 -> x1, local copies, waits for them, and re-layouts: 4.87 us -> 2.06 us
where the time goes in v2:
time: 77 us; the launch traced here: 76.1 us
  Pallas kernels  74 us (96%)
  local copies, waits for them, and re-layouts  2.06 us (3%)
    pallas_call x1, Pallas kernels, on_device(): pl.pallas_call(functools.partial(kernel, n), out_shape=jax.ShapeDtypeStru...  74 us
    unnamed x1, local copies, waits for them, and re-layouts  2.06 us

profile of v2, /device:TPU:0, one launch (start us, length us, event | category | flops | bytes accessed | tf_op | source)
XLA Modules:
  0.0 76.1 jit_solution(11379470540098900279)
XLA Ops:
  0.0 74.0 %moe_ring.1 = bf16[128,3072]{1,0:T(8,128)(2,1)} custom-call(bf16[128,3072]{1,0:T(8,128)(2,1)} %tok_hbm.1, s32[2,128]{1,0:T(2,128)} %bitcast.2, f32[2,128]{1,0:T(2,128)} %bitcast.3, bf16[1,3072,2048]{2,1,0:T(8,128)(2,1)} %w_gate.1, bf16[1,3072,2048]{2,1,0:T(8,128)(2,1)} %w_up.1, bf16[1,2048,3072]{2,1,0:T(8,128)(2,1)} %w_down.1), custom_call_target="tpu_custom_call" | custom-call | tf_op jit(solution)/shard_map/moe_ring/pallas_call | solution.py:286
  74.0 2.1 %copy.8 = bf16[128,3072]{1,0:T(8,128)(2,1)} copy(bf16[128,3072]{1,0:T(8,128)(2,1)} %moe_ring.1) | data formatting | bytes 1572864

commit v3 on v2

--- a/solution.py
+++ b/solution.py
@@ -66,18 +66,18 @@
     gather = jnp.concatenate(pieces, axis=0)
     brought[2].wait()
     loads = []
-    for at, (src, dst) in enumerate(((w_gate, wg), (w_up, wu), (w_down, wd))):
-        rows = dst.shape[0] // 2
-        pair = []
-        for k in range(2):
-            copy = pltpu.make_async_copy(src.at[0, pl.ds(k * rows, rows)], dst.at[pl.ds(k * rows, rows)], w_sem.at[at, k])
-            copy.start()
-            pair.append(copy)
-        loads.append(pair)
-    buf = jnp.dot(gather.astype(jnp.bfloat16), tok[...], preferred_element_type=jnp.float32).astype(jnp.bfloat16)
-    x[0, 0, 0] = buf[:CAP]
-    stage[0] = buf[CAP:]
-
+
+    def load_start():
+        for at, (src, dst) in enumerate(((w_gate, wg), (w_up, wu), (w_down, wd))):
+            rows = dst.shape[0] // 2
+            pair = []
+            for k in range(2):
+                copy = pltpu.make_async_copy(src.at[0, pl.ds(k * rows, rows)], dst.at[pl.ds(k * rows, rows)], w_sem.at[at, k])
+                copy.start()
+                pair.append(copy)
+            loads.append(pair)
+
+    chosen = gather.astype(jnp.bfloat16)
     pl.semaphore_wait(barrier, 5)
 
     started = []
@@ -90,6 +90,9 @@
         return x.at[t // 2, t % 2, d, :, pl.ds(s * width, width)]
 
     def ag_copy(t, d, s):
+        if t == 1 and d == 1:
+            return remote(stage.at[0, :, pl.ds(s * width, width)], xref(1, 1, s), ag_send.at[d, t, s], ag_recv.at[d, t, s],
+                          {"cuts": left, "expert": other})
         if t == 1:
             src = xref(0, d, s)
         elif t == half + 1:
@@ -103,14 +106,18 @@
         copy.start()
         started.append(copy)
 
+    for s in range(SUB):
+        cols = slice(s * width, (s + 1) * width)
+        buf = jnp.dot(chosen, tok[:, cols], preferred_element_type=jnp.float32).astype(jnp.bfloat16)
+        x[0, 0, 0, :, cols] = buf[:CAP]
+        stage[0, :, cols] = buf[CAP:]
+        ag_start(1, 0, s)
+        ag_start(1, 1, s)
     swap = remote(stage.at[0], x.at[0, 0, 1], swap_send.at[0], swap_recv.at[0], {"expert": other})
     swap.start()
     started.append(swap)
-    for s in range(SUB):
-        ag_start(1, 0, s)
+    load_start()
     swap.wait_recv()
-    for s in range(SUB):
-        ag_start(1, 1, s)
 
     def ag(t, s):
         for d in range(2):
@@ -239,7 +246,7 @@
                 advance(t if s == SUB - 1 else t - 1)
     while opened == 0:
         advance(n - 1)
-    for k in range(half - 2, -1, -1):
+    for k in range(half - 2, 0, -1):
         for s in range(SUB):
             rs(0, k, s)
             advance(n - 1)
@@ -260,6 +267,7 @@
     outs = []
     for s in range(SUB):
         cols = slice(s * width, (s + 1) * width)
+        rs(0, 0, s)
         rs(1, 0, s)
         first = fin[0, 0, :, cols].astype(jnp.float32) + fin[0, 1, :, cols].astype(jnp.float32) + part[0, 0, 0, :, cols].astype(jnp.float32)
         second = fin[1, 0, :, cols].astype(jnp.float32) + fin[1, 1, :, cols].astype(jnp.float32) + stage[1, :, cols].astype(jnp.float32)

time: 77 us -> 73.7 us (0.957); the launches traced: 76.1 us -> 73.5 us
  Pallas kernels: 74 us -> 71.5 us
    pallas_call x1, Pallas kernels: 74 us -> 71.5 us  [on_device(): pl.pallas_call(functools.partial(kernel, n), out_shape=jax.ShapeDtypeStru...]
where the time goes in v3:
time: 73.7 us; the launch traced here: 73.5 us
  Pallas kernels  71.5 us (97%)
  local copies, waits for them, and re-layouts  2.06 us (3%)
    pallas_call x1, Pallas kernels, on_device(): pl.pallas_call(functools.partial(kernel, n), out_shape=jax.ShapeDtypeStru...  71.5 us
    unnamed x1, local copies, waits for them, and re-layouts  2.06 us

profile of v3, /device:TPU:0, one launch (start us, length us, event | category | flops | bytes accessed | tf_op | source)
XLA Modules:
  0.0 73.5 jit_solution(17324941832234541761)
XLA Ops:
  0.0 71.5 %moe_ring.1 = bf16[128,3072]{1,0:T(8,128)(2,1)} custom-call(bf16[128,3072]{1,0:T(8,128)(2,1)} %tok_hbm.1, s32[2,128]{1,0:T(2,128)} %bitcast.2, f32[2,128]{1,0:T(2,128)} %bitcast.3, bf16[1,3072,2048]{2,1,0:T(8,128)(2,1)} %w_gate.1, bf16[1,3072,2048]{2,1,0:T(8,128)(2,1)} %w_up.1, bf16[1,2048,3072]{2,1,0:T(8,128)(2,1)} %w_down.1), custom_call_target="tpu_custom_call" | custom-call | tf_op jit(solution)/shard_map/moe_ring/pallas_call | solution.py:294
  71.5 2.1 %copy.8 = bf16[128,3072]{1,0:T(8,128)(2,1)} copy(bf16[128,3072]{1,0:T(8,128)(2,1)} %moe_ring.1) | data formatting | bytes 1572864

commit v4 on v3

--- a/solution.py
+++ b/solution.py
@@ -12,7 +12,7 @@
 TILE = 512
 UP_BITS = 2
 DOWN_BITS = 2
-WARM = 3
+WARM = 2
 MESH = pl.DeviceIdType.MESH
 
 
@@ -69,13 +69,11 @@
 
     def load_start():
         for at, (src, dst) in enumerate(((w_gate, wg), (w_up, wu), (w_down, wd))):
-            rows = dst.shape[0] // 2
-            pair = []
-            for k in range(2):
-                copy = pltpu.make_async_copy(src.at[0, pl.ds(k * rows, rows)], dst.at[pl.ds(k * rows, rows)], w_sem.at[at, k])
-                copy.start()
-                pair.append(copy)
-            loads.append(pair)
+            cols = dst.shape[1] // 2
+            loads.append([pltpu.make_async_copy(src.at[0, :, pl.ds(k * cols, cols)], dst.at[:, pl.ds(k * cols, cols)], w_sem.at[at, k])
+                          for k in range(2)])
+        for at, k in ((0, 0), (1, 0), (0, 1), (1, 1), (2, 0), (2, 1)):
+            loads[at][k].start()
 
     chosen = gather.astype(jnp.bfloat16)
     pl.semaphore_wait(barrier, 5)
@@ -129,10 +127,9 @@
                 ag_start(half + 1, d, s)
 
     def up_part(j, lo, hi):
-        if j == 0 and lo == 0:
+        if j == 0:
             for pair in loads[:2]:
-                for copy in pair:
-                    copy.wait()
+                pair[0 if lo == 0 else 1].wait()
 
         def body(c, carry):
             cols = pl.ds(pl.multiple_of(c * TILE, TILE), TILE)
@@ -146,9 +143,8 @@
         lax.fori_loop(lo, hi, body, 0)
 
     def down_part(j, lo, hi):
-        if j == 0 and lo == 0:
-            for copy in loads[2]:
-                copy.wait()
+        if j == 0:
+            loads[2][0 if lo == 0 else 1].wait()
 
         def body(c, carry):
             cols = pl.ds(pl.multiple_of(c * TILE, TILE), TILE)

time: 73.7 us -> 75.9 us (1.030)
  Pallas kernels: 71.5 us -> 73.7 us
    pallas_call x1, Pallas kernels: 71.5 us -> 73.7 us  [on_device(): pl.pallas_call(functools.partial(kernel, n), out_shape=jax.ShapeDtypeStru...]
where the time goes in v4:
time: 75.9 us; the launch traced here: 75.7 us
  Pallas kernels  73.7 us (97%)
  local copies, waits for them, and re-layouts  2.06 us (3%)
    pallas_call x1, Pallas kernels, on_device(): pl.pallas_call(functools.partial(kernel, n), out_shape=jax.ShapeDtypeStru...  73.7 us
    unnamed x1, local copies, waits for them, and re-layouts  2.06 us

profile of v4, /device:TPU:0, one launch (start us, length us, event | category | flops | bytes accessed | tf_op | source)
XLA Modules:
  0.0 75.7 jit_solution(13915814992535307207)
XLA Ops:
  0.0 73.7 %moe_ring.1 = bf16[128,3072]{1,0:T(8,128)(2,1)} custom-call(bf16[128,3072]{1,0:T(8,128)(2,1)} %tok_hbm.1, s32[2,128]{1,0:T(2,128)} %bitcast.2, f32[2,128]{1,0:T(2,128)} %bitcast.3, bf16[1,3072,2048]{2,1,0:T(8,128)(2,1)} %w_gate.1, bf16[1,3072,2048]{2,1,0:T(8,128)(2,1)} %w_up.1, bf16[1,2048,3072]{2,1,0:T(8,128)(2,1)} %w_down.1), custom_call_target="tpu_custom_call" | custom-call | tf_op jit(solution)/shard_map/moe_ring/pallas_call | solution.py:290
  73.7 2.1 %copy.8 = bf16[128,3072]{1,0:T(8,128)(2,1)} copy(bf16[128,3072]{1,0:T(8,128)(2,1)} %moe_ring.1) | data formatting | bytes 1572864
